TPU v7x, 32 devices: a whole 2x2x4 slice. The times are simulated.
32 devices in a mesh: groups: 2 (over y), feat: 4 (over z), dp: 4 (over x, core).
Axes of the slice: x: 2, y: 2, z: 4, core: 2. Of those that a mesh axis runs over, the one named last changes fastest.
Arguments:
- features: bfloat16 [2048, 8192], P(('groups', 'dp'), 'feat'), parts along dimension 0, may hold values from -6 to 6
- bn_gain: float32 [8192], P('feat'), may hold values from 0.1 to 1.9
- bn_shift: float32 [8192], P('feat'), may hold values from -0.5 to 0.5
- weight: bfloat16 [8192, 8192], P('feat'), may hold values from -2 to 2
Outputs:
- covariance: float32 [16384, 8192], P(('groups', 'dp'), 'feat'), parts along dimension 0
- grad_in: bfloat16 [2048, 8192], P(('groups', 'dp'), 'feat'), parts along dimension 0
There are 2 independent parts, one for each index of `groups`. A program takes and returns all parts, laid end to end along the dimension named above; an argument that names none is the same for every part. Nothing has to cross between parts.
All inputs are finite; a program needn't handle non-finite values.
Results may differ from a plain program's by a relative error of at most 0.014.
Values may be sent and summed in bfloat16 or wider, within the bound.
A program may use at most 256 MiB of HBM per device.

v0:
```python
import jax
import jax.numpy as jnp
from jax import lax
from jax.sharding import PartitionSpec as P


def swap(value, distance):
    count = lax.axis_size("dp")
    return lax.ppermute(value, "dp", [(i, i ^ distance) for i in range(count)])


def block_order(count):
    order = [0]
    bit = count // 2
    while bit:
        order = order + [o ^ bit for o in order]
        bit //= 2
    return order


def gather_rows(value):
    bit = lax.axis_size("dp") // 2
    while bit:
        value = jnp.concatenate([value, swap(value, bit)], 0)
        bit //= 2
    return value


def column_blocks(full):
    count = lax.axis_size("dp")
    width = full.shape[1] // count
    me = lax.axis_index("dp")
    return [lax.dynamic_slice_in_dim(full, (me ^ o) * width, width, 1) for o in block_order(count)]


def exchange(blocks):
    order = block_order(lax.axis_size("dp"))
    return jnp.concatenate([swap(b, o) if o else b for b, o in zip(blocks, order)], 0)


def shards(features, bn_gain, bn_shift, weight):
    dp_count = lax.axis_size("dp")
    feat_count = lax.axis_size("feat")
    local_rows = features.shape[0]
    images = local_rows * dp_count
    hidden = features.astype(jnp.float32)
    col_sums, col_squares = lax.psum((jnp.sum(hidden, 0), jnp.sum(hidden * hidden, 0)), "dp")
    mean_h = col_sums / images
    var_h = col_squares / images - mean_h * mean_h
    normed = (hidden - mean_h) * lax.rsqrt(var_h + 1e-05) * bn_gain + bn_shift
    activated = jnp.maximum(normed, 0.0).astype(jnp.bfloat16)
    partial_value = jnp.dot(activated, weight, preferred_element_type=jnp.float32).astype(
        jnp.bfloat16
    )
    proj_f = lax.psum_scatter(partial_value, "feat", scatter_dimension=1, tiled=True).astype(
        jnp.float32
    )
    proj_mean = lax.psum(jnp.sum(proj_f, 0), "dp") / images
    centered = (proj_f - proj_mean).astype(jnp.bfloat16)
    cent_full = lax.all_gather(centered, "feat", axis=1, tiled=True)
    piece = gather_rows(centered)
    gram = lax.dot_general(
        centered, piece, (((1,), (1,)), ((), ())), preferred_element_type=jnp.float32
    )
    piece_f = piece.astype(jnp.float32)
    proj_var = jnp.sum(piece_f * piece_f, 0) / (images - 1)
    spread = jnp.sqrt(proj_var + 0.0001)
    scale_up = images / (images - 1)
    active = jnp.where(spread < 1.0, 1.0 / spread, 0.0)
    factor = lax.all_gather(
        4.0 * scale_up * proj_var + 25.0 * scale_up * active, "feat", axis=0, tiled=True
    )
    cent_full, factor, _ = lax.optimization_barrier((cent_full, factor, gram))
    gram = lax.psum(gram, "feat")
    cent_full, cuts = lax.optimization_barrier((cent_full, column_blocks(cent_full)))
    cent_x = exchange(cuts)
    scaled = (cent_full.astype(jnp.float32) * factor).astype(jnp.bfloat16)
    dims = (((1,), (1,)), ((), ()))
    through = lax.dot_general(cent_full, weight, dims, preferred_element_type=jnp.float32)
    direct = lax.dot_general(scaled, weight, dims, preferred_element_type=jnp.float32)
    through_all = gather_rows(through.astype(jnp.bfloat16))
    covariance = lax.dot_general(
        cent_x, piece, (((0,), (0,)), ((), ())), preferred_element_type=jnp.float32
    ) / (images - 1)
    gram, covariance = lax.optimization_barrier((gram, covariance))
    own = jnp.arange(local_rows, dtype=jnp.int32)[:, None]
    same = own == jnp.arange(images, dtype=jnp.int32)[None, :]
    gram = gram * (4.0 * scale_up / (images - 1))
    diag = jnp.sum(jnp.where(same, gram, 0.0), 1, keepdims=True)
    rest = jnp.where(same, 0.0, gram).astype(jnp.bfloat16)
    grad_in = (
        jnp.dot(rest, through_all, preferred_element_type=jnp.float32) + diag * through - direct
    )
    return (covariance, grad_in.astype(jnp.bfloat16))


def solution(mesh):
    in_specs = (P(("groups", "dp"), "feat"), P("feat"), P("feat"), P("feat", None))
    out_specs = (P(("groups", "dp"), "feat"), P(("groups", "dp"), "feat"))
    return jax.shard_map(shards, mesh=mesh, in_specs=in_specs, out_specs=out_specs, check_vma=False)
```

profile of v0, /device:TPU:0, one launch (start us, length us, event | category | flops | bytes accessed | tf_op | source)
XLA Modules:
  0.0 327.4 jit_solution(5208170377373880028)
XLA Ops:
  7.2 0.0 reduce-scatter.2.cloned.1.call-start
  7.2 1.5 convert_reduce_fusion
  8.7 12.7 %all-reduce = (f32[2048]{0:T(1024)S(1)}, f32[2048]{0:T(1024)S(1)}) all-reduce(f32[2048]{0:T(1024)S(1)} %get-tuple-element.21, f32[2048]{0:T(1024)S(1)} %get-tuple-element.20), channel_id=1, replica_groups=mesh['groups'=2,'feat'=4,'dp'=4] {'dp'}, use_global_device_ids=true, to_apply=%region_3.0 | all-reduce | flops 4096 | bytes 32768 | tf_op jit(solution)/shard_map/psum | solution.py:47
  21.4 16.7 %convolution_convert_fusion = bf16[256,8192]{1,0:T(8,128)(2,1)} fusion(bf16[2048,8192]{1,0:T(8,128)(2,1)} %param.7, bf16[256,2048]{1,0:T(8,128)(2,1)} %param.4, f32[2048]{0:T(1024)} %param.6, f32[2048]{0:T(1024)} %param.5, f32[2048]{0:T(1024)S(1)} %get-tuple-element.29, f32[2048]{0:T(1024)S(1)} %get-tuple-element.28), kind=kOutput, calls=%fused_computation | convolution fusion | flops 8595701760 | bytes 38830080 | tf_op jit(solution)/shard_map/dot_general | solution.py:52
  38.1 0.0 reduce-scatter.2.cloned.1.call-update
  38.2 0.0 all-gather.2.cloned.1.call-start
  38.2 77.2 %reduce-scatter.2.cloned.1.call-done = bf16[256,2048]{1,0:T(8,128)(2,1)} async-done(((bf16[256,8192]{1,0:T(8,128)(2,1)}), bf16[256,2048]{1,0:T(8,128)(2,1)}) %reduce-scatter.2.cloned.1.call-update) | async-done | bytes 1048592 | tf_op jit(solution)/shard_map/reduce_scatter | solution.py:55
  115.4 1.4 convert_reduce_fusion.1
  116.8 7.0 %psum.30 = f32[2048]{0:T(1024)S(1)} all-reduce(f32[2048]{0:T(1024)S(1)} %convert_reduce_fusion.1), channel_id=1, replica_groups=mesh['groups'=2,'feat'=4,'dp'=4] {'dp'}, use_global_device_ids=true, to_apply=%region_6.0 | all-reduce | flops 2048 | bytes 16384 | tf_op jit(solution)/shard_map/psum | solution.py:58
  123.8 2.4 fusion.24
  126.3 0.0 copy-start
  126.3 0.0 all-gather.2.cloned.1.call-update
  126.3 0.0 all-reduce.3.cloned.1.call-start
  126.3 0.6 collective-permute-start
  126.9 23.4 %collective-permute-done = bf16[256,2048]{1,0:T(8,128)(2,1)S(1)} collective-permute-done((bf16[256,2048]{1,0:T(8,128)(2,1)}, bf16[256,2048]{1,0:T(8,128)(2,1)S(1)}, u32[]{:S(2)}, u32[]{:S(2)}) %collective-permute-start) | collective-permute-done | bytes 1048608 | tf_op jit(solution)/shard_map/ppermute | solution.py:9
  150.3 2.8 pad_maximum_fusion.1
  153.1 0.0 collective-permute-start.1
  153.1 4.5 %collective-permute-done.1 = bf16[512,2048]{1,0:T(8,128)(2,1)} collective-permute-done((bf16[512,2048]{1,0:T(8,128)(2,1)}, bf16[512,2048]{1,0:T(8,128)(2,1)}, u32[]{:S(2)}, u32[]{:S(2)}) %collective-permute-start.1) | collective-permute-done | bytes 2097184 | tf_op jit(solution)/shard_map/ppermute | solution.py:9
  157.6 0.0 copy-done
  157.6 2.2 multiply_reduce_fusion
  159.8 15.5 %all_gather.7 = f32[8192]{0:T(1024)S(1)} all-gather(f32[2048]{0:T(1024)S(1)} %multiply_add_fusion), channel_id=1, replica_groups=mesh['groups'=2,'feat'=4,'dp'=4] {'feat'}, dimensions={0}, use_global_device_ids=true | all-gather | bytes 40960 | tf_op jit(solution)/shard_map/all_gather | solution.py:70
  175.3 3.9 %fusion.44 = f32[256,1024]{1,0:T(8,128)} fusion(bf16[256,2048]{1,0:T(8,128)(2,1)S(1)} %copy-done, bf16[512,2048]{1,0:T(8,128)(2,1)} %collective-permute-done.1, bf16[256,2048]{1,0:T(8,128)(2,1)S(1)} %collective-permute-done), kind=kOutput, calls=%fused_computation.61 | convolution fusion | flops 1086324736 | bytes 5242880 | tf_op jit(solution)/shard_map/dot_general | solution.py:62
  179.2 28.0 %all-gather.2.cloned.1.call-done = bf16[256,8192]{1,0:T(8,128)(2,1)} async-done(((bf16[256,2048]{1,0:T(8,128)(2,1)}), bf16[256,8192]{1,0:T(8,128)(2,1)}) %all-gather.2.cloned.1.call-update) | async-done | bytes 4194320 | tf_op jit(solution)/shard_map/all_gather | solution.py:60
  207.2 4.0 %constant_dynamic-slice_fusion = (bf16[256,2048]{1,0:T(8,128)(2,1)}, bf16[256,2048]{1,0:T(8,128)(2,1)}, bf16[256,2048]{1,0:T(8,128)(2,1)}, bf16[256,2048]{1,0:T(8,128)(2,1)S(1)}) fusion(bf16[256,8192]{1,0:T(8,128)(2,1)} %all-gather.2.cloned.1.call-done, s32[]{:T(128)S(6)} %select_n.28, s32[]{:T(128)S(6)} %select_n.27, s32[]{:T(128)S(6)} %select_n.26, ...), kind=kLoop, calls=%fused_computation.52 | loop fusion | bytes 8388624 | tf_op jit(solution)/shard_map/dynamic_slice | solution.py:33
  211.2 17.4 %fusion.45 = (bf16[256,2048]{1,0:T(8,128)(2,1)}, f32[256,2048]{1,0:T(8,128)}) fusion(bf16[256,8192]{1,0:T(8,128)(2,1)} %all-gather.2.cloned.1.call-done, bf16[2048,8192]{1,0:T(8,128)(2,1)} %param.7), kind=kOutput, calls=%fused_computation.62 | convolution fusion | flops 8590458880 | bytes 40894464 | tf_op jit(solution)/shard_map/dot_general | solution.py:79
  228.6 1.5 collective-permute-start.5
  230.0 0.0 all-reduce.3.cloned.1.call-update
  230.1 0.1 collective-permute-start.4
  230.1 0.7 collective-permute-start.3
  230.8 1.5 collective-permute-start.2
  232.3 22.7 %collective-permute-done.5 = bf16[256,2048]{1,0:T(8,128)(2,1)} collective-permute-done((bf16[256,2048]{1,0:T(8,128)(2,1)}, bf16[256,2048]{1,0:T(8,128)(2,1)}, u32[]{:S(2)}, u32[]{:S(2)}) %collective-permute-start.5) | collective-permute-done | bytes 1048608 | tf_op jit(solution)/shard_map/ppermute | solution.py:9
  254.9 3.2 pad_maximum_fusion.2
  258.1 0.0 collective-permute-start.6
  258.1 17.3 %fusion = f32[256,2048]{1,0:T(8,128)} fusion(bf16[2048,8192]{1,0:T(8,128)(2,1)} %param.7, bf16[256,8192]{1,0:T(8,128)(2,1)} %all-gather.2.cloned.1.call-done, f32[8192]{0:T(1024)S(1)} %all_gather.7), kind=kOutput, calls=%fused_computation.4 | convolution fusion | flops 8596226048 | bytes 39878656 | tf_op jit(solution)/shard_map/dot_general | solution.py:80
  275.4 1.0 collective-permute-done.4
  276.4 0.0 collective-permute-done.3
  276.4 22.3 %collective-permute-done.2 = bf16[256,2048]{1,0:T(8,128)(2,1)} collective-permute-done((bf16[256,2048]{1,0:T(8,128)(2,1)}, bf16[256,2048]{1,0:T(8,128)(2,1)}, u32[]{:S(2)}, u32[]{:S(2)}) %collective-permute-start.2) | collective-permute-done | bytes 1048608 | tf_op jit(solution)/shard_map/ppermute | solution.py:9
  298.7 14.7 %convolution_multiply_fusion = f32[2048,2048]{1,0:T(8,128)} fusion(bf16[256,2048]{1,0:T(8,128)(2,1)} %collective-permute-done.4, bf16[256,2048]{1,0:T(8,128)(2,1)} %collective-permute-done.3, bf16[256,2048]{1,0:T(8,128)(2,1)} %collective-permute-done.2, bf16[256,2048]{1,0:T(8,128)(2,1)S(1)} %get-tuple-element.12, ...), kind=kOutput, calls=%fused_computation.1 | convolution fusion | flops 8623489024 | bytes 25165824 | tf_op jit(solution)/shard_map/dot_general | solution.py:82
  313.4 0.0 all-reduce.3.cloned.1.call-done
  313.4 1.3 select_reduce_fusion
  314.7 0.0 collective-permute-done.6
  314.8 6.1 %fusion.21 = bf16[256,2048]{1,0:T(8,128)(2,1)} fusion(f32[256,2048]{1,0:T(8,128)} %fusion, bf16[512,2048]{1,0:T(8,128)(2,1)} %collective-permute-done.6, bf16[256,2048]{1,0:T(8,128)(2,1)} %collective-permute-done.5, bf16[256,2048]{1,0:T(8,128)(2,1)} %get-tuple-element.30, f32[256,2048]{1,0:T(8,128)} %get-tuple-element.31, f32[256]{0:T(256)S(1)} %select_reduce_fusion, ...), kind=kOutput, calls=%fused_computation.27 | convolution fusion | flops 1089470464 | bytes 10486784 | tf_op jit(solution)/shard_map/dot_general | solution.py:92
  (3 shorter events, 0.0 us)
Async XLA Ops:
  7.2 108.3 %reduce-scatter.2.cloned.1.call-start = ((), (), s32[]{:S(2)}) async-start(), calls=%async_computation.1 | async-start | bytes 5242880 | tf_op jit(solution)/shard_map/reduce_scatter | solution.py:55
  38.2 169.0 %all-gather.2.cloned.1.call-start = ((), (), s32[]{:S(2)}) async-start(), calls=%async_computation.3 | async-start | bytes 5242880 | tf_op jit(solution)/shard_map/all_gather | solution.py:60
  126.3 31.4 %copy-start = (bf16[256,2048]{1,0:T(8,128)(2,1)S(1)}, bf16[256,2048]{1,0:T(8,128)(2,1)}, u32[]{:S(2)}) copy-start(bf16[256,2048]{1,0:T(8,128)(2,1)} %fusion.24) | copy-start | bytes 3145732
  126.3 187.1 %all-reduce.3.cloned.1.call-start = ((), (), s32[]{:S(2)}) async-start(), calls=%async_computation.2 | async-start | bytes 2097152 | tf_op jit(solution)/shard_map/psum | solution.py:74
  126.3 24.0 %collective-permute-start = (bf16[256,2048]{1,0:T(8,128)(2,1)}, bf16[256,2048]{1,0:T(8,128)(2,1)S(1)}, u32[]{:S(2)}, u32[]{:S(2)}) collective-permute-start(bf16[256,2048]{1,0:T(8,128)(2,1)} %fusion.24), channel_id=1, source_target_pairs={{0,2},{1,3},{2,0},{3,1},{4,6},{5,7},{6,4},{7,5},{8,10},{9,11},{10,... | collective-permute-start | bytes 3145736 | tf_op jit(solution)/shard_map/ppermute | solution.py:9
  153.1 4.5 %collective-permute-start.1 = (bf16[512,2048]{1,0:T(8,128)(2,1)}, bf16[512,2048]{1,0:T(8,128)(2,1)}, u32[]{:S(2)}, u32[]{:S(2)}) collective-permute-start(bf16[512,2048]{1,0:T(8,128)(2,1)} %pad_maximum_fusion.1), channel_id=1, source_target_pairs={{0,1},{1,0},{2,3},{3,2},{4,5},{5,4},{6,7},{7,6},{8,9},{9,8},{10,11... | collective-permute-start | bytes 6291464 | tf_op jit(solution)/shard_map/ppermute | solution.py:9
  228.6 26.4 %collective-permute-start.5 = (bf16[256,2048]{1,0:T(8,128)(2,1)}, bf16[256,2048]{1,0:T(8,128)(2,1)}, u32[]{:S(2)}, u32[]{:S(2)}) collective-permute-start(bf16[256,2048]{1,0:T(8,128)(2,1)} %get-tuple-element.30), channel_id=1, source_target_pairs={{0,2},{1,3},{2,0},{3,1},{4,6},{5,7},{6,4},{7,5},{8,10},{9,11},{10,... | collective-permute-start | bytes 3145736 | tf_op jit(solution)/shard_map/ppermute | solution.py:9
  230.1 46.3 %collective-permute-start.4 = (bf16[256,2048]{1,0:T(8,128)(2,1)}, bf16[256,2048]{1,0:T(8,128)(2,1)}, u32[]{:S(2)}, u32[]{:S(2)}) collective-permute-start(bf16[256,2048]{1,0:T(8,128)(2,1)} %get-tuple-element.15), channel_id=1, source_target_pairs={{0,3},{1,2},{2,1},{3,0},{4,7},{5,6},{6,5},{7,4},{8,11},{9,10},{10,... | collective-permute-start | bytes 3145736 | tf_op jit(solution)/shard_map/ppermute | solution.py:9
  230.1 46.3 %collective-permute-start.3 = (bf16[256,2048]{1,0:T(8,128)(2,1)}, bf16[256,2048]{1,0:T(8,128)(2,1)}, u32[]{:S(2)}, u32[]{:S(2)}) collective-permute-start(bf16[256,2048]{1,0:T(8,128)(2,1)} %get-tuple-element.14), channel_id=1, source_target_pairs={{0,1},{1,0},{2,3},{3,2},{4,5},{5,4},{6,7},{7,6},{8,9},{9,8},{10,11... | collective-permute-start | bytes 3145736 | tf_op jit(solution)/shard_map/ppermute | solution.py:9
  230.8 67.9 %collective-permute-start.2 = (bf16[256,2048]{1,0:T(8,128)(2,1)}, bf16[256,2048]{1,0:T(8,128)(2,1)}, u32[]{:S(2)}, u32[]{:S(2)}) collective-permute-start(bf16[256,2048]{1,0:T(8,128)(2,1)} %get-tuple-element.13), channel_id=1, source_target_pairs={{0,2},{1,3},{2,0},{3,1},{4,6},{5,7},{6,4},{7,5},{8,10},{9,11},{10,... | collective-permute-start | bytes 3145736 | tf_op jit(solution)/shard_map/ppermute | solution.py:9
  258.1 56.7 %collective-permute-start.6 = (bf16[512,2048]{1,0:T(8,128)(2,1)}, bf16[512,2048]{1,0:T(8,128)(2,1)}, u32[]{:S(2)}, u32[]{:S(2)}) collective-permute-start(bf16[512,2048]{1,0:T(8,128)(2,1)} %pad_maximum_fusion.2), channel_id=1, source_target_pairs={{0,1},{1,0},{2,3},{3,2},{4,5},{5,4},{6,7},{7,6},{8,9},{9,8},{10,11... | collective-permute-start | bytes 6291464 | tf_op jit(solution)/shard_map/ppermute | solution.py:9
Sparse Core Ops, SparseCore 0:
  38.3 77.0 reduce-scatter.1
  126.4 80.7 all-gather.1
  230.2 49.4 all-reduce.2
where the time goes:
time: 328 us; the launch traced here: 327 us
  waiting for transfers between devices  179 us (55%)
  matrix products  76.1 us (23%)
  blocking collectives  35.1 us (11%)
  other arithmetic  14.9 us (5%)
  between operations  13.8 us (4%)
  starting transfers between devices  4.41 us (1%)
  local copies, waits for them, and re-layouts  3.97 us (1%)
    reduce_scatter x1, waiting for transfers between devices, shards(): lax.psum_scatter(partial_value, 'feat', scatter_dimension=1, tiled=True)  77.2 us
    ppermute x7, waiting for transfers between devices, swap(): return lax.ppermute(value, 'dp', [(i, i ^ distance) for i in range(count)])  73.9 us
    all_gather x1, waiting for transfers between devices, shards(): cent_full = lax.all_gather(centered, 'feat', axis=1, tiled=True)  28 us
    dot_general x1, matrix products, shards(): lax.dot_general(cent_full, weight, dims, preferred_element_type=jnp.float32)  17.4 us
    dot_general x1, matrix products, shards(): lax.dot_general(scaled, weight, dims, preferred_element_type=jnp.float32)  17.3 us
    dot_general x1, matrix products, shards(): jnp.dot(activated, weight, preferred_element_type=jnp.float32)  16.7 us
    all_gather x1, blocking collectives, shards(): lax.all_gather(4.0 * scale_up * proj_var + 25.0 * scale_up * active, 'fea...  15.5 us
    dot_general x1, matrix products, shards(): lax.dot_general(cent_x, piece, (((0,), (0,)), ((), ())), preferred_elemen...  14.7 us
  transfers between devices with their start and end apart: 10, of which 7 were waited for; matrix products, arithmetic and copies ran while one was open for 14% of the time, Pallas kernels for 0%

commit v1 on v0

--- a/solution.py
+++ b/solution.py
@@ -57,7 +57,12 @@
     )
     proj_mean = lax.psum(jnp.sum(proj_f, 0), "dp") / images
     centered = (proj_f - proj_mean).astype(jnp.bfloat16)
-    cent_full = lax.all_gather(centered, "feat", axis=1, tiled=True)
+    ring = [centered]
+    for hop in range(3):
+        ring.append(lax.ppermute(ring[-1], "feat", [(dev, (dev + 1) % 4) for dev in range(4)]))
+    cent_full = jnp.roll(
+        jnp.concatenate(ring[::-1], axis=1), (lax.axis_index("feat") + 1) * ring[0].shape[1], axis=1
+    )
     piece = gather_rows(centered)
     gram = lax.dot_general(
         centered, piece, (((1,), (1,)), ((), ())), preferred_element_type=jnp.float32

time: 328 us -> 340 us (1.037)
  waiting for transfers between devices: 179 us -> 187 us
  local copies, waits for them, and re-layouts: 3.97 us -> 10.6 us
  starting transfers between devices: 4.41 us -> 8.68 us
  other arithmetic: 14.9 us -> 11.5 us
    ppermute x0 -> x3, waiting for transfers between devices: none -> 69.5 us  [shards(): lax.ppermute(ring[-1], 'feat', [(dev, (dev + 1) % 4) for dev in range(4)])]
    ppermute x7, waiting for transfers between devices: 73.9 us -> 40.1 us  [swap(): return lax.ppermute(value, 'dp', [(i, i ^ distance) for i in range(count)])]
    all_gather x1 -> x0, waiting for transfers between devices: 28 us -> none  [shards(): cent_full = lax.all_gather(centered, 'feat', axis=1, tiled=True)]
    unnamed x2 -> x16, local copies, waits for them, and re-layouts: 0.01 us -> 3.86 us
  transfers between devices with their start and end apart: 10 -> 12, of which waited for: 7 -> 7; matrix products, arithmetic and copies ran while one was open for 14% -> 12% of each run, Pallas kernels for 0% -> 0%
where the time goes in v1:
time: 340 us
  waiting for transfers between devices  187 us (55%)
  matrix products  75.2 us (22%)
  blocking collectives  32.8 us (10%)
  between operations  14.2 us (4%)
  other arithmetic  11.5 us (3%)
  local copies, waits for them, and re-layouts  10.6 us (3%)
  starting transfers between devices  8.68 us (3%)
    reduce_scatter x1, waiting for transfers between devices, shards(): lax.psum_scatter(partial_value, 'feat', scatter_dimension=1, tiled=True)  77.2 us
    ppermute x3, waiting for transfers between devices, shards(): lax.ppermute(ring[-1], 'feat', [(dev, (dev + 1) % 4) for dev in range(4)])  69.5 us
    ppermute x7, waiting for transfers between devices, swap(): return lax.ppermute(value, 'dp', [(i, i ^ distance) for i in range(count)])  40.1 us
    dot_general x1, matrix products, shards(): lax.dot_general(scaled, weight, dims, preferred_element_type=jnp.float32)  17.4 us
    dot_general x1, matrix products, shards(): lax.dot_general(cent_full, weight, dims, preferred_element_type=jnp.float32)  17 us
    dot_general x1, matrix products, shards(): jnp.dot(activated, weight, preferred_element_type=jnp.float32)  16.7 us
    dot_general x1, matrix products, shards(): lax.dot_general(cent_x, piece, (((0,), (0,)), ((), ())), preferred_elemen...  14.5 us
    all_gather x1, blocking collectives, shards(): lax.all_gather(4.0 * scale_up * proj_var + 25.0 * scale_up * active, 'fea...  13.1 us
  transfers between devices with their start and end apart: 12, of which 7 were waited for; matrix products, arithmetic and copies ran while one was open for 12% of the time, Pallas kernels for 0%

profile of v1, /device:TPU:0, one launch (start us, length us, event | category | flops | bytes accessed | tf_op | source)
XLA Modules:
  0.0 339.8 jit_solution(2377157389512464793)
XLA Ops:
  7.2 0.0 reduce-scatter.2.cloned.1.call-start
  7.2 1.5 convert_reduce_fusion
  8.7 12.7 %all-reduce = (f32[2048]{0:T(1024)S(1)}, f32[2048]{0:T(1024)S(1)}) all-reduce(f32[2048]{0:T(1024)S(1)} %get-tuple-element.21, f32[2048]{0:T(1024)S(1)} %get-tuple-element.20), channel_id=1, replica_groups=mesh['groups'=2,'feat'=4,'dp'=4] {'dp'}, use_global_device_ids=true, to_apply=%region_3.0 | all-reduce | flops 4096 | bytes 32768 | tf_op jit(solution)/shard_map/psum | solution.py:47
  21.4 16.7 %convolution_convert_fusion = bf16[256,8192]{1,0:T(8,128)(2,1)} fusion(bf16[2048,8192]{1,0:T(8,128)(2,1)} %param.7, bf16[256,2048]{1,0:T(8,128)(2,1)} %param.4, f32[2048]{0:T(1024)} %param.6, f32[2048]{0:T(1024)} %param.5, f32[2048]{0:T(1024)S(1)} %get-tuple-element.29, f32[2048]{0:T(1024)S(1)} %get-tuple-element.28), kind=kOutput, calls=%fused_computation | convolution fusion | flops 8595701760 | bytes 38830080 | tf_op jit(solution)/shard_map/dot_general | solution.py:52
  38.1 0.0 reduce-scatter.2.cloned.1.call-update
  38.2 0.0 all-reduce.3.cloned.1.call-start
  38.2 77.2 %reduce-scatter.2.cloned.1.call-done = bf16[256,2048]{1,0:T(8,128)(2,1)} async-done(((bf16[256,8192]{1,0:T(8,128)(2,1)}), bf16[256,2048]{1,0:T(8,128)(2,1)}) %reduce-scatter.2.cloned.1.call-update) | async-done | bytes 1048592 | tf_op jit(solution)/shard_map/reduce_scatter | solution.py:55
  115.4 1.4 convert_reduce_fusion.1
  116.8 7.0 %psum.30 = f32[2048]{0:T(1024)S(1)} all-reduce(f32[2048]{0:T(1024)S(1)} %convert_reduce_fusion.1), channel_id=1, replica_groups=mesh['groups'=2,'feat'=4,'dp'=4] {'dp'}, use_global_device_ids=true, to_apply=%region_6.0 | all-reduce | flops 2048 | bytes 16384 | tf_op jit(solution)/shard_map/psum | solution.py:58
  123.8 1.4 fusion.24
  125.3 1.5 collective-permute-start.2
  126.8 24.1 %collective-permute-done.2 = bf16[256,2048]{1,0:T(8,128)(2,1)S(1)} collective-permute-done((bf16[256,2048]{1,0:T(8,128)(2,1)S(1)}, bf16[256,2048]{1,0:T(8,128)(2,1)S(1)}, u32[]{:S(2)}, u32[]{:S(2)}) %collective-permute-start.2) | collective-permute-done | bytes 1048608 | tf_op jit(solution)/shard_map/ppermute | solution.py:62
  150.8 0.0 collective-permute-start.3
  150.8 1.5 collective-permute-start
  152.3 23.1 %collective-permute-done.3 = bf16[256,2048]{1,0:T(8,128)(2,1)S(1)} collective-permute-done((bf16[256,2048]{1,0:T(8,128)(2,1)S(1)}, bf16[256,2048]{1,0:T(8,128)(2,1)S(1)}, u32[]{:S(2)}, u32[]{:S(2)}) %collective-permute-start.3) | collective-permute-done | bytes 1048608 | tf_op jit(solution)/shard_map/ppermute | solution.py:62
  175.4 0.0 collective-permute-start.4
  175.4 0.0 collective-permute-done
  175.4 1.4 pad_maximum_fusion.1
  176.8 0.0 copy-start
  176.8 0.1 collective-permute-start.1
  176.9 22.3 %collective-permute-done.4 = bf16[256,2048]{1,0:T(8,128)(2,1)} collective-permute-done((bf16[256,2048]{1,0:T(8,128)(2,1)S(1)}, bf16[256,2048]{1,0:T(8,128)(2,1)}, u32[]{:S(2)}, u32[]{:S(2)}) %collective-permute-start.4) | collective-permute-done | bytes 1048608 | tf_op jit(solution)/shard_map/ppermute | solution.py:62
  199.2 1.3 constant_dynamic-update-slice_fusion.7
  200.5 0.1 constant_dynamic-update-slice_fusion.6
  200.6 0.1 constant_dynamic-update-slice_fusion.5
  200.6 0.0 copy-done
  200.7 0.2 constant_dynamic-update-slice_fusion.4
  200.9 1.3 constant_dynamic-update-slice_fusion.3
  202.2 0.1 constant_dynamic-update-slice_fusion.2
  202.3 0.1 constant_dynamic-update-slice_fusion.1
  202.3 0.2 constant_dynamic-update-slice_fusion
  202.6 2.3 constant_dynamic-slice_fusion.4
  204.9 0.0 collective-permute-done.1
  204.9 0.0 copy-start.1
  204.9 2.4 multiply_reduce_fusion
  207.3 13.1 %all_gather.3 = f32[8192]{0:T(1024)S(1)} all-gather(f32[2048]{0:T(1024)S(1)} %multiply_add_fusion), channel_id=1, replica_groups=mesh['groups'=2,'feat'=4,'dp'=4] {'feat'}, dimensions={0}, use_global_device_ids=true | all-gather | bytes 40960 | tf_op jit(solution)/shard_map/all_gather | solution.py:75
  220.5 0.0 copy-done.1
  220.5 3.5 %fusion.44 = f32[256,1024]{1,0:T(8,128)} fusion(bf16[256,2048]{1,0:T(8,128)(2,1)S(1)} %fusion.24, bf16[512,2048]{1,0:T(8,128)(2,1)S(1)} %collective-permute-done.1, bf16[256,2048]{1,0:T(8,128)(2,1)} %collective-permute-done), kind=kOutput, calls=%fused_computation.70 | convolution fusion | flops 1086324736 | bytes 5242880 | tf_op jit(solution)/shard_map/dot_general | solution.py:67
  224.0 4.4 %constant_dynamic-slice_fusion = (bf16[256,2048]{1,0:T(8,128)(2,1)}, bf16[256,2048]{1,0:T(8,128)(2,1)}, bf16[256,2048]{1,0:T(8,128)(2,1)}, bf16[256,2048]{1,0:T(8,128)(2,1)}) fusion(bf16[256,8192]{1,0:T(8,128)(2,1)} %constant_dynamic-slice_fusion.4, s32[]{:T(128)S(6)} %select_n.43, s32[]{:T(128)S(6)} %select_n.42, s32[]{:T(128)S(6)} %select_n.41, ...), kind=kLoop, calls=%fused_computation.60 | loop fusion | bytes 8388624 | tf_op jit(solution)/shard_map/dynamic_slice | solution.py:33
  228.3 17.0 %fusion.45 = (bf16[256,2048]{1,0:T(8,128)(2,1)S(1)}, f32[256,2048]{1,0:T(8,128)}) fusion(bf16[256,8192]{1,0:T(8,128)(2,1)} %constant_dynamic-slice_fusion.4, bf16[2048,8192]{1,0:T(8,128)(2,1)} %param.7), kind=kOutput, calls=%fused_computation.71 | convolution fusion | flops 8590458880 | bytes 40894464 | tf_op jit(solution)/shard_map/dot_general | solution.py:84
  245.4 0.0 copy-start.3
  245.4 3.3 collective-permute-start.8
  248.7 0.0 all-reduce.3.cloned.1.call-update
  248.7 0.1 collective-permute-start.7
  248.8 0.1 collective-permute-start.6
  248.9 2.0 collective-permute-start.5
  251.0 21.8 %collective-permute-done.8 = bf16[256,2048]{1,0:T(8,128)(2,1)S(1)} collective-permute-done((bf16[256,2048]{1,0:T(8,128)(2,1)S(1)}, bf16[256,2048]{1,0:T(8,128)(2,1)S(1)}, u32[]{:S(2)}, u32[]{:S(2)}) %collective-permute-start.8) | collective-permute-done | bytes 1048608 | tf_op jit(solution)/shard_map/ppermute | solution.py:9
  272.8 0.0 copy-done.3
  272.8 0.0 copy-start.4
  272.8 1.0 copy-done.4
  273.8 1.5 pad_maximum_fusion.2
  275.3 0.0 copy-start.2
  275.3 0.0 collective-permute-start.9
  275.3 17.4 %fusion = f32[256,2048]{1,0:T(8,128)} fusion(bf16[2048,8192]{1,0:T(8,128)(2,1)} %param.7, bf16[256,8192]{1,0:T(8,128)(2,1)} %constant_dynamic-slice_fusion.4, f32[8192]{0:T(1024)S(1)} %all_gather.3), kind=kOutput, calls=%fused_computation.4 | convolution fusion | flops 8596226048 | bytes 39878656 | tf_op jit(solution)/shard_map/dot_general | solution.py:85
  292.7 2.2 collective-permute-done.7
  294.9 0.0 collective-permute-done.6
  294.9 16.1 %collective-permute-done.5 = bf16[256,2048]{1,0:T(8,128)(2,1)} collective-permute-done((bf16[256,2048]{1,0:T(8,128)(2,1)}, bf16[256,2048]{1,0:T(8,128)(2,1)}, u32[]{:S(2)}, u32[]{:S(2)}) %collective-permute-start.5) | collective-permute-done | bytes 1048608 | tf_op jit(solution)/shard_map/ppermute | solution.py:9
  311.0 0.0 copy-done.2
  311.0 14.5 %convolution_multiply_fusion = f32[2048,2048]{1,0:T(8,128)} fusion(bf16[256,2048]{1,0:T(8,128)(2,1)} %collective-permute-done.7, bf16[256,2048]{1,0:T(8,128)(2,1)} %collective-permute-done.6, bf16[256,2048]{1,0:T(8,128)(2,1)} %collective-permute-done.5, bf16[256,2048]{1,0:T(8,128)(2,1)} %get-tuple-element.12, bf16[512,2048]{1,0:T(8,128)(2,1)S(1)} %copy-done.2, ...), kind=kOutput, calls=%fused_computation.1 | convolution fusion | flops 8623489024 | bytes 25165824 | tf_op jit(solution)/shard_map/dot_general | solution.py:87
  325.5 0.0 all-reduce.3.cloned.1.call-done
  325.5 1.3 select_reduce_fusion
  326.8 0.0 collective-permute-done.9
  326.8 6.1 %fusion.21 = bf16[256,2048]{1,0:T(8,128)(2,1)} fusion(f32[256,2048]{1,0:T(8,128)} %fusion, bf16[512,2048]{1,0:T(8,128)(2,1)} %collective-permute-done.9, bf16[256,2048]{1,0:T(8,128)(2,1)} %copy-done.4, bf16[256,2048]{1,0:T(8,128)(2,1)} %copy-done.3, f32[256,2048]{1,0:T(8,128)} %get-tuple-element.31, f32[256]{0:T(256)S(1)} %select_reduce_fusion, ...), kind=kOutput, calls=%fused_computation.27 | convolution fusion | flops 1089470464 | bytes 10486784 | tf_op jit(solution)/shard_map/dot_general | solution.py:97
  (3 shorter events, 0.0 us)
Async XLA Ops:
  7.2 108.3 %reduce-scatter.2.cloned.1.call-start = ((), (), s32[]{:S(2)}) async-start(), calls=%async_computation.1 | async-start | bytes 5242880 | tf_op jit(solution)/shard_map/reduce_scatter | solution.py:55
  38.2 287.3 %all-reduce.3.cloned.1.call-start = ((), (), s32[]{:S(2)}) async-start(), calls=%async_computation.2 | async-start | bytes 2097152 | tf_op jit(solution)/shard_map/psum | solution.py:79
  125.3 25.6 %collective-permute-start.2 = (bf16[256,2048]{1,0:T(8,128)(2,1)S(1)}, bf16[256,2048]{1,0:T(8,128)(2,1)S(1)}, u32[]{:S(2)}, u32[]{:S(2)}) collective-permute-start(bf16[256,2048]{1,0:T(8,128)(2,1)S(1)} %fusion.24), channel_id=1, source_target_pairs={{0,4},{4,8},{8,12},{12,0},{1,5},{5,9},{9,13},{13,1},{2,6},{6,10},{... | collective-permute-start | bytes 3145736 | tf_op jit(solution)/shard_map/ppermute | solution.py:62
  150.8 24.6 %collective-permute-start.3 = (bf16[256,2048]{1,0:T(8,128)(2,1)S(1)}, bf16[256,2048]{1,0:T(8,128)(2,1)S(1)}, u32[]{:S(2)}, u32[]{:S(2)}) collective-permute-start(bf16[256,2048]{1,0:T(8,128)(2,1)S(1)} %collective-permute-done.2), channel_id=1, source_target_pairs={{0,4},{4,8},{8,12},{12,0},{1,5},{5,9},{9,13},{13,1},{2,6},{6,10},{... | collective-permute-start | bytes 3145736 | tf_op jit(solution)/shard_map/ppermute | solution.py:62
  150.8 24.6 %collective-permute-start = (bf16[256,2048]{1,0:T(8,128)(2,1)S(1)}, bf16[256,2048]{1,0:T(8,128)(2,1)}, u32[]{:S(2)}, u32[]{:S(2)}) collective-permute-start(bf16[256,2048]{1,0:T(8,128)(2,1)S(1)} %fusion.24), channel_id=1, source_target_pairs={{0,2},{1,3},{2,0},{3,1},{4,6},{5,7},{6,4},{7,5},{8,10},{9,11},{10,... | collective-permute-start | bytes 3145736 | tf_op jit(solution)/shard_map/ppermute | solution.py:9
  175.4 23.8 %collective-permute-start.4 = (bf16[256,2048]{1,0:T(8,128)(2,1)S(1)}, bf16[256,2048]{1,0:T(8,128)(2,1)}, u32[]{:S(2)}, u32[]{:S(2)}) collective-permute-start(bf16[256,2048]{1,0:T(8,128)(2,1)S(1)} %collective-permute-done.3), channel_id=1, source_target_pairs={{0,4},{4,8},{8,12},{12,0},{1,5},{5,9},{9,13},{13,1},{2,6},{6,10},{... | collective-permute-start | bytes 3145736 | tf_op jit(solution)/shard_map/ppermute | solution.py:62
  176.8 23.8 %copy-start = (bf16[256,2048]{1,0:T(8,128)(2,1)S(1)}, bf16[256,2048]{1,0:T(8,128)(2,1)}, u32[]{:S(2)}) copy-start(bf16[256,2048]{1,0:T(8,128)(2,1)} %reduce-scatter.2.cloned.1.call-done) | copy-start | bytes 3145732
  176.8 28.1 %collective-permute-start.1 = (bf16[512,2048]{1,0:T(8,128)(2,1)S(1)}, bf16[512,2048]{1,0:T(8,128)(2,1)S(1)}, u32[]{:S(2)}, u32[]{:S(2)}) collective-permute-start(bf16[512,2048]{1,0:T(8,128)(2,1)S(1)} %pad_maximum_fusion.1), channel_id=1, source_target_pairs={{0,1},{1,0},{2,3},{3,2},{4,5},{5,4},{6,7},{7,6},{8,9},{9,8},{10,11... | collective-permute-start | bytes 6291464 | tf_op jit(solution)/shard_map/ppermute | solution.py:9
  204.9 15.6 %copy-start.1 = (bf16[512,2048]{1,0:T(8,128)(2,1)}, bf16[512,2048]{1,0:T(8,128)(2,1)S(1)}, u32[]{:S(2)}) copy-start(bf16[512,2048]{1,0:T(8,128)(2,1)S(1)} %collective-permute-done.1) | copy-start | bytes 6291460
  245.4 27.4 %copy-start.3 = (bf16[256,2048]{1,0:T(8,128)(2,1)}, bf16[256,2048]{1,0:T(8,128)(2,1)S(1)}, u32[]{:S(2)}) copy-start(bf16[256,2048]{1,0:T(8,128)(2,1)S(1)} %get-tuple-element.30) | copy-start | bytes 3145732
  245.4 27.4 %collective-permute-start.8 = (bf16[256,2048]{1,0:T(8,128)(2,1)S(1)}, bf16[256,2048]{1,0:T(8,128)(2,1)S(1)}, u32[]{:S(2)}, u32[]{:S(2)}) collective-permute-start(bf16[256,2048]{1,0:T(8,128)(2,1)S(1)} %get-tuple-element.30), channel_id=1, source_target_pairs={{0,2},{1,3},{2,0},{3,1},{4,6},{5,7},{6,4},{7,5},{8,10},{9,11},{10,... | collective-permute-start | bytes 3145736 | tf_op jit(solution)/shard_map/ppermute | solution.py:9
  248.7 46.2 %collective-permute-start.7 = (bf16[256,2048]{1,0:T(8,128)(2,1)}, bf16[256,2048]{1,0:T(8,128)(2,1)}, u32[]{:S(2)}, u32[]{:S(2)}) collective-permute-start(bf16[256,2048]{1,0:T(8,128)(2,1)} %get-tuple-element.15), channel_id=1, source_target_pairs={{0,3},{1,2},{2,1},{3,0},{4,7},{5,6},{6,5},{7,4},{8,11},{9,10},{10,... | collective-permute-start | bytes 3145736 | tf_op jit(solution)/shard_map/ppermute | solution.py:9
  248.8 46.1 %collective-permute-start.6 = (bf16[256,2048]{1,0:T(8,128)(2,1)}, bf16[256,2048]{1,0:T(8,128)(2,1)}, u32[]{:S(2)}, u32[]{:S(2)}) collective-permute-start(bf16[256,2048]{1,0:T(8,128)(2,1)} %get-tuple-element.14), channel_id=1, source_target_pairs={{0,1},{1,0},{2,3},{3,2},{4,5},{5,4},{6,7},{7,6},{8,9},{9,8},{10,11... | collective-permute-start | bytes 3145736 | tf_op jit(solution)/shard_map/ppermute | solution.py:9
  248.9 62.1 %collective-permute-start.5 = (bf16[256,2048]{1,0:T(8,128)(2,1)}, bf16[256,2048]{1,0:T(8,128)(2,1)}, u32[]{:S(2)}, u32[]{:S(2)}) collective-permute-start(bf16[256,2048]{1,0:T(8,128)(2,1)} %get-tuple-element.13), channel_id=1, source_target_pairs={{0,2},{1,3},{2,0},{3,1},{4,6},{5,7},{6,4},{7,5},{8,10},{9,11},{10,... | collective-permute-start | bytes 3145736 | tf_op jit(solution)/shard_map/ppermute | solution.py:9
  272.8 1.0 copy-start.4
  275.3 35.7 %copy-start.2 = (bf16[512,2048]{1,0:T(8,128)(2,1)S(1)}, bf16[512,2048]{1,0:T(8,128)(2,1)}, u32[]{:S(2)}) copy-start(bf16[512,2048]{1,0:T(8,128)(2,1)} %copy-done.1) | copy-start | bytes 6291460
  275.3 51.5 %collective-permute-start.9 = (bf16[512,2048]{1,0:T(8,128)(2,1)}, bf16[512,2048]{1,0:T(8,128)(2,1)}, u32[]{:S(2)}, u32[]{:S(2)}) collective-permute-start(bf16[512,2048]{1,0:T(8,128)(2,1)} %pad_maximum_fusion.2), channel_id=1, source_target_pairs={{0,1},{1,0},{2,3},{3,2},{4,5},{5,4},{6,7},{7,6},{8,9},{9,8},{10,11... | collective-permute-start | bytes 6291464 | tf_op jit(solution)/shard_map/ppermute | solution.py:9
Sparse Core Ops, SparseCore 0:
  38.3 77.0 reduce-scatter.1
  248.9 49.0 all-reduce.2
